TPU v7x, 256 devices: a whole 4x4x8 slice. The times are simulated.
256 devices in a mesh: mem: 32 (over z, x), fsdp: 8 (over y, core).
Axes of the slice: x: 4, y: 4, z: 8, core: 2. Of those that a mesh axis runs over, the one named last changes fastest.
Arguments:
- layer_input: bfloat16 [32768, 4096], P(('mem', 'fsdp')), may hold values from -6 to 6
- w_query: bfloat16 [4096, 2048], P('mem', 'fsdp'), may hold values from -0.09375 to 0.09375
- local_kv: bfloat16 [2, 32768, 2048], P(None, 'mem', 'fsdp'), may hold values from -200 to 200, as said below
- memory_kv: bfloat16 [512, 2, 128, 2048], P('mem', None, None, 'fsdp'), may hold values from -200 to 200
- memory_ids: int32 [256, 4], P('mem'), may hold values from 0 to 511, as said below
- grad_out: bfloat16 [32768, 2048], P('mem', 'fsdp'), may hold values from -6 to 6
Outputs:
- attended: bfloat16 [32768, 2048], P('mem', 'fsdp')
- grad_input: bfloat16 [32768, 4096], P(('mem', 'fsdp'))
Inputs may be any that keep to these rules, and one draw needn't show every extreme that they name: `memory_ids`: within the tiles of one local context (8 tiles), all named blocks of one owner (same id // 16) are one and the same block, and every owner is named by some tile of every local context; each tile names 4 blocks of different owners. `local_kv`: keys and values of the document's tokens.
All inputs are finite; a program needn't handle non-finite values.
Results may differ from a plain program's by a relative error of at most 0.025.
The roundings to bfloat16 on the way count: a program that leaves them out, or rounds other values in their place, can miss the bound.
Values may be sent and summed in bfloat16 or wider, within the bound.
No kernel may reach another device: no remote copies, remote signals or barrier semaphores. Data moves between devices by JAX's collectives and lax.ppermute only.
A program may use at most 128 MiB of HBM per device.

v0:
```python
import math

import jax
import jax.numpy as jnp
from jax import lax
from jax.sharding import Mesh
from jax.sharding import PartitionSpec as P

HD = 128
BLK = 128
TOPK = 4
MB_DEV = 16
MEM = ("mem_0", "mem_1")
MEM_FSDP = ("mem_0", "mem_1", "fsdp")


NEG_FILL = -1e30


def gather_axes(x, axes, dim):
    if not axes:
        return x
    nearer = lax.all_gather(x, axes[-1], axis=dim, tiled=True)
    return gather_axes(nearer, axes[:-1], dim)


def attend_context(queries, context_kv, tile_kv, grad_rows):
    ctx_len, width = queries.shape
    heads_count = width // HD
    tiles_count = tile_kv.shape[0]
    mem_keys_count = TOPK * BLK
    score_scale = 1.0 / math.sqrt(HD)
    query_heads = queries.reshape(ctx_len, heads_count, HD)
    query_tiles = query_heads.reshape(tiles_count, BLK, heads_count, HD)
    local_keys = context_kv[0].reshape(ctx_len, heads_count, HD)
    local_values = context_kv[1].reshape(ctx_len, heads_count, HD)
    mem_keys = tile_kv[:, :, 0].reshape(tiles_count, mem_keys_count, heads_count, HD)
    mem_values = tile_kv[:, :, 1].reshape(tiles_count, mem_keys_count, heads_count, HD)
    grad_heads = grad_rows.reshape(ctx_len, heads_count, HD)
    grad_tiles = grad_heads.reshape(tiles_count, BLK, heads_count, HD)
    mem_scores = (
        jnp.einsum("tqhd,tkhd->htqk", query_tiles, mem_keys, preferred_element_type=jnp.float32)
        * score_scale
    )
    mem_scores = mem_scores.reshape(heads_count, ctx_len, mem_keys_count)
    loc_scores = (
        jnp.einsum("qhd,khd->hqk", query_heads, local_keys, preferred_element_type=jnp.float32)
        * score_scale
    )
    positions = jnp.arange(ctx_len, dtype=jnp.int32)
    causal = positions[:, None] >= positions[None, :]
    loc_scores = jnp.where(causal[None], loc_scores, NEG_FILL)
    row_max = jnp.maximum(jnp.max(mem_scores, axis=2), jnp.max(loc_scores, axis=2))
    mem_exp = jnp.exp(mem_scores - row_max[:, :, None])
    loc_exp = jnp.exp(loc_scores - row_max[:, :, None])
    total = jnp.sum(mem_exp, axis=2) + jnp.sum(loc_exp, axis=2)
    mem_prob = mem_exp / total[:, :, None]
    loc_prob = loc_exp / total[:, :, None]
    mem_weights = mem_prob.astype(jnp.bfloat16).reshape(
        heads_count, tiles_count, BLK, mem_keys_count
    )
    loc_weights = loc_prob.astype(jnp.bfloat16)
    mem_part = jnp.einsum(
        "htqk,tkhd->tqhd", mem_weights, mem_values, preferred_element_type=jnp.float32
    )
    loc_part = jnp.einsum(
        "hqk,khd->qhd", loc_weights, local_values, preferred_element_type=jnp.float32
    )
    attended = (
        (mem_part.reshape(ctx_len, heads_count, HD) + loc_part)
        .reshape(ctx_len, width)
        .astype(jnp.bfloat16)
    )
    mem_dprob = jnp.einsum(
        "tqhd,tkhd->htqk", grad_tiles, mem_values, preferred_element_type=jnp.float32
    )
    mem_dprob = mem_dprob.reshape(heads_count, ctx_len, mem_keys_count)
    loc_dprob = jnp.einsum(
        "qhd,khd->hqk", grad_heads, local_values, preferred_element_type=jnp.float32
    )
    delta = jnp.sum(mem_prob * mem_dprob, axis=2) + jnp.sum(loc_prob * loc_dprob, axis=2)
    mem_dscore = (mem_prob * (mem_dprob - delta[:, :, None])).astype(jnp.bfloat16)
    loc_dscore = (loc_prob * (loc_dprob - delta[:, :, None])).astype(jnp.bfloat16)
    mem_dscore = mem_dscore.reshape(heads_count, tiles_count, BLK, mem_keys_count)
    mem_grad = jnp.einsum(
        "htqk,tkhd->tqhd", mem_dscore, mem_keys, preferred_element_type=jnp.float32
    )
    loc_grad = jnp.einsum(
        "hqk,khd->qhd", loc_dscore, local_keys, preferred_element_type=jnp.float32
    )
    grad_queries = ((mem_grad.reshape(ctx_len, heads_count, HD) + loc_grad) * score_scale).reshape(
        ctx_len, width
    )
    return (attended, grad_queries.astype(jnp.bfloat16))


def local(layer_input, w_query, local_kv, memory_kv, memory_ids, grad_out):
    owners_count = lax.axis_size(MEM)
    owner_of = memory_ids // MB_DEV
    owner_range = jnp.arange(owners_count, dtype=jnp.int32)
    matches = owner_of[:, :, None] == owner_range[None, None, :]
    local_index = (memory_ids % MB_DEV)[:, :, None]
    wanted_local = jnp.max(jnp.where(matches, local_index, 0), axis=(0, 1)).reshape(owners_count, 1)
    asked = lax.all_to_all(wanted_local, MEM, split_axis=0, concat_axis=0, tiled=True)
    outgoing = jnp.take(memory_kv, asked[:, 0], axis=0)
    received = lax.all_to_all(outgoing, MEM, split_axis=0, concat_axis=0, tiled=True)
    tile_kv = jnp.take(received, owner_of, axis=0)
    weight_slice = gather_axes(w_query, MEM, 0)
    queries = jnp.dot(
        lax.all_gather(layer_input, "fsdp", axis=0, tiled=True),
        weight_slice,
        preferred_element_type=jnp.float32,
    ).astype(jnp.bfloat16)
    attended, grad_queries = attend_context(queries, local_kv, tile_kv, grad_out)
    grad_input = lax.psum_scatter(
        lax.dot_general(
            grad_queries, weight_slice, (((1,), (1,)), ((), ())), preferred_element_type=jnp.float32
        ).astype(jnp.bfloat16),
        "fsdp",
        scatter_dimension=0,
        tiled=True,
    )
    return (attended, grad_input)


def solution(mesh):
    torus = Mesh(mesh.devices.reshape(8, 4, mesh.shape["fsdp"]), ("mem_0", "mem_1", "fsdp"))
    in_specs = (
        P(MEM_FSDP, None),
        P(MEM, "fsdp"),
        P(None, MEM, "fsdp"),
        P(MEM, None, None, "fsdp"),
        P(MEM, None),
        P(MEM, "fsdp"),
    )
    out_specs = (P(MEM, "fsdp"), P(MEM_FSDP, None))
    return jax.shard_map(local, mesh=torus, in_specs=in_specs, out_specs=out_specs, check_vma=False)
```

profile of v0, /device:TPU:129, one launch (start us, length us, event | category | flops | bytes accessed | tf_op | source)
XLA Modules:
  0.0 267.6 jit_solution(203501331925917594)
XLA Ops:
  7.2 0.0 copy-start
  7.2 0.0 all-gather.5.cloned.1.call-start
  7.2 11.7 %all_gather.10 = bf16[512,256]{1,0:T(8,128)(2,1)} all-gather(bf16[128,256]{1,0:T(8,128)(2,1)} %param.7), channel_id=1, replica_groups=mesh['mem_0'=8,'mem_1'=4,'fsdp'=8] {'mem_1'}, dimensions={0}, use_global_device_ids=true | all-gather | bytes 327680 | tf_op jit(solution)/shard_map/all_gather | solution.py:23
  18.9 0.0 all-gather.5.cloned.1.call-update
  19.0 0.0 all-gather.3.cloned.1.call-start
  19.0 0.7 all-gather.3.cloned.1.call-update
  19.7 0.7 add_select_fusion
  20.4 0.7 compare_and_fusion.1
  21.1 0.1 select_reduce_fusion
  21.2 0.1 copy.111
  21.3 11.4 %all_to_all.20 = s32[32,1,1]{2,1,0:T(1,128)S(1)} all-to-all(s32[32,1,1]{2,1,0:T(1,128)S(1)} %copy.111), channel_id=1, replica_groups=mesh['mem_0'=8,'mem_1'=4,'fsdp'=8] {'mem_0','mem_1'}, dimensions={0} | all-to-all | bytes 256 | tf_op jit(solution)/shard_map/all_to_all | solution.py:104
  32.7 0.7 reduce.3
  33.4 0.0 copy-done
  33.4 2.7 %gather_fusion = bf16[32,2,128,256]{3,2,1,0:T(8,128)(2,1)} fusion(bf16[16,2,128,256]{3,2,1,0:T(8,128)(2,1)S(1)} %copy-done, s32[1024]{0:T(1024)S(1)} %pad_clamp_fusion.1), kind=kCustom, calls=%fused_computation | custom fusion | bytes 8388736 | tf_op jit(solution)/shard_map/jit(_take)/gather | solution.py:105
  36.1 4.6 %broadcast_select_fusion = bf16[32,2,128,256]{3,2,1,0:T(8,128)(2,1)} fusion(bf16[32,2,128,256]{3,2,1,0:T(8,128)(2,1)} %gather_fusion, pred[32]{0:T(512)(128)(4,1)S(1)} %compare_and_fusion), kind=kLoop, calls=%fused_computation.22 | loop fusion | flops 2097152 | bytes 8388640 | tf_op jit(solution)/shard_map/jit(_take)/select_n | solution.py:105
  40.8 9.6 %all-to-all-start.1 = ((bf16[32,2,128,256]{3,2,1,0:T(8,128)(2,1)}), bf16[32,2,128,256]{3,2,1,0:T(8,128)(2,1)}, u32[]{:S(2)}, u32[]{:S(2)}) async-start(bf16[32,2,128,256]{3,2,1,0:T(8,128)(2,1)} %broadcast_select_fusion), calls=%async_computation.1 | async-start | bytes 8388608 | tf_op jit(solution)/shard_map/all_to_all | solution.py:106
  50.4 0.0 copy-start.7
  50.4 0.0 reduce-scatter.2.cloned.1.call-start
  50.4 0.1 copy.112
  50.5 0.1 reshape.139
  50.6 0.1 copy.110
  50.7 0.0 copy-done.6
  50.7 0.1 fusion.56
  50.8 1.0 copy.142
  51.8 1.0 copy.122
  52.8 0.0 copy-done.7
  52.8 0.9 reshape_reshape.7
  53.7 0.3 iota_compare_fusion
  54.0 90.9 %all-to-all-done.1 = bf16[32,2,128,256]{3,2,1,0:T(8,128)(2,1)} async-done(((bf16[32,2,128,256]{3,2,1,0:T(8,128)(2,1)}), bf16[32,2,128,256]{3,2,1,0:T(8,128)(2,1)}, u32[]{:S(2)}, u32[]{:S(2)}) %all-to-all-start.1) | async-done | bytes 4194336 | tf_op jit(solution)/shard_map/all_to_all | solution.py:106
  144.9 4.9 %gather_fusion.1 = bf16[32,2,128,256]{3,2,1,0:T(8,128)(2,1)} fusion(bf16[32,2,128,256]{3,2,1,0:T(8,128)(2,1)} %all-to-all-done.1, s32[1024]{0:T(1024)S(1)} %pad_clamp_fusion), kind=kCustom, calls=%fused_computation.1 | custom fusion | bytes 8388736 | tf_op jit(solution)/shard_map/jit(_take)/gather | solution.py:107
  149.8 2.7 %copy_select_fusion = bf16[8,4,2,128,256]{4,3,1,0,2:T(8,128)(2,1)S(1)} fusion(bf16[8,4,2,128,256]{4,3,2,1,0:T(8,128)(2,1)} %bitcast.89, pred[8,4]{1,0:T(8,128)(4,1)S(1)} %copy.110), kind=kLoop, calls=%fused_computation.16 | loop fusion | flops 2097152 | bytes 8388640 | tf_op jit(solution)/shard_map/jit(_take)/select_n | solution.py:107
  152.5 2.3 fusion.55
  154.8 2.5 reshape_squeeze.13
  157.3 4.0 %reshape_squeeze.12 = bf16[8,512,2,128]{3,2,1,0:T(2,128)(2,1)} reshape(bf16[8,4,1,128,256]{4,3,1,0,2:T(8,128)(2,1)} %get-tuple-element.17) | data formatting | bytes 4194304 | tf_op jit(solution)/shard_map/reshape;squeeze | solution.py:38
  161.3 6.3 %convolution_convert_fusion.1 = bf16[1024,256]{0,1:T(8,128)(2,1)S(1)} fusion(bf16[1024,4096]{1,0:T(8,128)(2,1)} %all-gather.3.cloned.1.call-done, bf16[4096,256]{1,0:T(8,128)(2,1)} %all-gather.5.cloned.1.call-done), kind=kOutput, calls=%fused_computation.44 | convolution fusion | flops 2147745792 | bytes 11010048 | tf_op jit(solution)/shard_map/dot_general | solution.py:109
  167.6 0.0 copy-start.10
  167.7 0.1 copy.144
  167.8 0.9 multiply_reduce_fusion.1
  168.6 0.0 copy-done.10
  168.7 2.0 fusion
  170.7 0.0 copy-start.2
  170.7 2.0 fusion.2
  172.8 0.0 copy-start.8
  172.8 0.0 copy-start.9
  172.8 1.3 fusion.11
  174.1 0.0 copy-done.2
  174.1 0.1 copy-done.8
  174.2 0.6 copy-done.9
  174.7 5.4 %multiply_reduce_fusion = (f32[2,1024]{1,0:T(2,128)S(1)}, f32[2,1024,1024]{1,2,0:T(8,128)}) fusion(f32[2,1024]{1,0:T(2,128)S(1)} %bitcast_add_fusion.2, f32[2,1024]{1,0:T(2,128)S(1)} %bitcast_maximum_fusion, f32[2,1024,1024]{1,2,0:T(8,128)S(1)} %get-tuple-element.23, pred[1024,1024]{0,1:T(8,128)(4,1)S(1)} %iota_compare_fusion, ...), kind=kOutput, calls=%fused_computation.3 | convolution fusion | flops 549451776 | bytes 18898944 | tf_op jit(solution)/shard_map/qhd,khd->hqk/dot_general | solution.py:78
  180.1 2.0 fusion.4
  182.1 2.4 fusion.6
  184.5 0.7 fusion.27
  185.3 0.1 copy.132
  185.3 1.3 copy.134
  186.6 9.6 %fusion.41 = bf16[1024,2,128]{0,2,1:T(8,128)(2,1)S(1)} fusion(f32[1024,2,128]{0,2,1:T(8,128)} %copy.134, bf16[1024,2,128]{0,2,1:T(8,128)(2,1)} %bitcast.96, f32[2,1024,1024]{1,2,0:T(8,128)} %get-tuple-element.27, f32[2,1024]{1,0:T(2,128)S(1)} %bitcast_add_fusion, f32[2,1024,1024]{1,2,0:T(8,128)} %copy-done.2, f32[2,1024]{1,0:T(2,128)S(1)} %bitcast_add_fusion.2, ...), kind=kOutput, calls=%fused_computation.43 | convolution fusion | flops 552337408 | bytes 19947520 | tf_op jit(solution)/shard_map/hqk,khd->qhd/dot_general | solution.py:88
  196.3 5.6 %convolution_convert_fusion = bf16[1024,4096]{1,0:T(8,128)(2,1)} fusion(bf16[1024,256]{0,1:T(8,128)(2,1)S(1)} %bitcast.93, bf16[4096,256]{1,0:T(8,128)(2,1)S(1)} %copy-done.3), kind=kOutput, calls=%fused_computation.6 | convolution fusion | flops 2151677952 | bytes 11010048 | tf_op jit(solution)/shard_map/dot_general | solution.py:116
  201.9 0.0 reduce-scatter.2.cloned.1.call-update
  202.0 1.6 copy-done.5
  203.5 2.3 fusion.22
  205.8 0.1 copy.121
  205.9 1.3 copy.124
  207.2 7.5 %fusion.42 = bf16[1024,2,128]{0,2,1:T(8,128)(2,1)} fusion(f32[1024,2,128]{0,2,1:T(8,128)} %copy.124, bf16[1024,2,128]{0,2,1:T(8,128)(2,1)} %bitcast.94, f32[2,1024,1024]{1,2,0:T(8,128)} %copy-done.2, f32[2,1024]{1,0:T(2,128)S(1)} %bitcast_add_fusion.2, f32[2,1024]{1,0:T(2,128)S(1)} %bitcast_maximum_fusion, pred[1024,1024]{0,1:T(8,128)(4,1)S(1)} %iota_compare_fusion), kind=kOutput, calls=%fused_computation.45 | convolution fusion | flops 547880960 | bytes 11550720 | tf_op jit(solution)/shard_map/hqk,khd->qhd/dot_general | solution.py:66
  214.7 2.0 copy.135
  216.8 44.3 %reduce-scatter.2.cloned.1.call-done = bf16[128,4096]{1,0:T(8,128)(2,1)} async-done(((bf16[1024,4096]{1,0:T(8,128)(2,1)}), bf16[128,4096]{1,0:T(8,128)(2,1)}) %reduce-scatter.2.cloned.1.call-update) | async-done | bytes 1048592 | tf_op jit(solution)/shard_map/reduce_scatter | solution.py:115
  (23 shorter events, 0.1 us)
Async XLA Ops:
  7.2 26.2 %copy-start = (bf16[16,2,128,256]{3,2,1,0:T(8,128)(2,1)S(1)}, bf16[16,2,128,256]{3,2,1,0:T(8,128)(2,1)}, u32[]{:S(2)}) copy-start(bf16[16,2,128,256]{3,2,1,0:T(8,128)(2,1)} %param.9) | copy-start | bytes 6291460
  7.2 154.1 %all-gather.5.cloned.1.call-start = ((), (), s32[]{:S(2)}) async-start(), calls=%async_computation.4 | async-start | bytes 2359296 | tf_op jit(solution)/shard_map/all_gather | solution.py:23
  19.0 142.3 %all-gather.3.cloned.1.call-start = ((), (), s32[]{:S(2)}) async-start(), calls=%async_computation.3 | async-start | bytes 9437184 | tf_op jit(solution)/shard_map/all_gather | solution.py:110
  40.8 9.9 %copy-start.6 = (bf16[2,1024,256]{2,1,0:T(8,128)(2,1)S(1)}, bf16[2,1024,256]{2,1,0:T(8,128)(2,1)}, u32[]{:S(2)}) copy-start(bf16[2,1024,256]{2,1,0:T(8,128)(2,1)} %param.8) | copy-start | bytes 3145732
  40.8 104.1 %all-to-all-start.1 = ((bf16[32,2,128,256]{3,2,1,0:T(8,128)(2,1)}), bf16[32,2,128,256]{3,2,1,0:T(8,128)(2,1)}, u32[]{:S(2)}, u32[]{:S(2)}) async-start(bf16[32,2,128,256]{3,2,1,0:T(8,128)(2,1)} %broadcast_select_fusion), calls=%async_computation.1 | async-start | bytes 8388608 | tf_op jit(solution)/shard_map/all_to_all | solution.py:106
  50.4 2.4 copy-start.7
  50.4 210.7 %reduce-scatter.2.cloned.1.call-start = ((), (), s32[]{:S(2)}) async-start(), calls=%async_computation.5 | async-start | bytes 9437184 | tf_op jit(solution)/shard_map/reduce_scatter | solution.py:115
  167.6 1.0 copy-start.10
  170.7 3.4 %copy-start.2 = (f32[2,1024,1024]{1,2,0:T(8,128)}, f32[2,1024,1024]{1,2,0:T(8,128)S(1)}, u32[]{:S(2)}) copy-start(f32[2,1024,1024]{1,2,0:T(8,128)S(1)} %get-tuple-element.23) | copy-start | bytes 25165828
  172.8 1.4 copy-start.8
  172.8 2.0 copy-start.9
  174.7 5.4 %copy-start.4 = (bf16[8,512,2,128]{3,2,1,0:T(2,128)(2,1)S(1)}, bf16[8,512,2,128]{3,2,1,0:T(2,128)(2,1)}, u32[]{:S(2)}) copy-start(bf16[8,512,2,128]{3,2,1,0:T(2,128)(2,1)} %reshape_squeeze.12) | copy-start | bytes 6291460
  174.7 5.4 %copy-start.11 = (bf16[8,128,2,128]{3,2,1,0:T(2,128)(2,1)S(1)}, bf16[8,128,2,128]{3,2,1,0:T(2,128)(2,1)}, u32[]{:S(2)}) copy-start(bf16[8,128,2,128]{3,2,1,0:T(2,128)(2,1)} %reshape_reshape.7) | copy-start | bytes 1572868
  186.6 9.7 %copy-start.3 = (bf16[4096,256]{1,0:T(8,128)(2,1)S(1)}, bf16[4096,256]{1,0:T(8,128)(2,1)}, u32[]{:S(2)}) copy-start(bf16[4096,256]{1,0:T(8,128)(2,1)} %all-gather.5.cloned.1.call-done) | copy-start | bytes 6291460
  201.9 1.6 copy-start.5
  207.2 53.9 %copy-start.1 = (bf16[16,2,128,256]{3,2,1,0:T(8,128)(2,1)S(1)}, bf16[16,2,128,256]{3,2,1,0:T(8,128)(2,1)}, u32[]{:S(2)}) copy-start(bf16[16,2,128,256]{3,2,1,0:T(8,128)(2,1)} %param.9) | copy-start | bytes 6291460
Sparse Core Ops, SparseCore 0:
  19.1 42.0 all-gather.4
  63.0 68.9 all-gather.2
  202.1 58.9 reduce-scatter.1
where the time goes:
time: 271 us; the launch traced here: 268 us
  waiting for transfers between devices  136 us (50%)
  matrix products  42.4 us (16%)
  local copies, waits for them, and re-layouts  27 us (10%)
  blocking collectives  23.1 us (9%)
  other arithmetic  15.5 us (6%)
  between operations  14 us (5%)
  starting transfers between devices  9.71 us (4%)
    all_to_all x1, waiting for transfers between devices, local(): lax.all_to_all(outgoing, MEM, split_axis=0, concat_axis=0, tiled=True)  90.9 us
    reduce_scatter x1, waiting for transfers between devices, local(): lax.psum_scatter(lax.dot_general(grad_queries, weight_slice, (((1,), (1,)...  44.3 us
    all_gather x1, blocking collectives, gather_axes(): nearer = lax.all_gather(x, axes[-1], axis=dim, tiled=True)  11.7 us
    all_to_all x1, blocking collectives, local(): lax.all_to_all(wanted_local, MEM, split_axis=0, concat_axis=0, tiled=True)  11.4 us
    dot_general x1, matrix products, attend_context(): jnp.einsum('hqk,khd->qhd', loc_dscore, local_keys, preferred_element_type...  9.64 us
    all_to_all x1, starting transfers between devices, local(): lax.all_to_all(outgoing, MEM, split_axis=0, concat_axis=0, tiled=True)  9.59 us
    dot_general x1, matrix products, attend_context(): jnp.einsum('hqk,khd->qhd', loc_weights, local_values, preferred_element_t...  7.54 us
    dot_general x1, matrix products, local(): jnp.dot(lax.all_gather(layer_input, 'fsdp', axis=0, tiled=True), weight_s...  6.35 us
  transfers between devices with their start and end apart: 4, of which 2 were waited for; matrix products, arithmetic and copies ran while one was open for 16% of the time, Pallas kernels for 0%

commit v1 on v0

v1 whole, which is shorter than its diff:
```python
import functools
import math

import jax
import jax.numpy as jnp
from jax import lax
from jax.experimental import pallas as pl
from jax.experimental.pallas import tpu as pltpu
from jax.sharding import Mesh
from jax.sharding import PartitionSpec as P

HD = 128
BLK = 128
TOPK = 4
MB_DEV = 16
CTX = 1024
TILES = CTX // BLK
ZN, XN, YN, CN = 8, 4, 4, 2
OWNERS = ZN * XN
HEADS = 2
WIDTH = HEADS * HD
DM = 4096
PAIR = 2 * BLK
MEM = ("z", "x")
VMEM_LIMIT = 40 * 1024 * 1024
NEG_FILL = -1e30


def dot(a, b, dims):
    return lax.dot_general(a, b, (dims, ((), ())), preferred_element_type=jnp.float32)


def pick_kernel(asked_ref, block_ref, *out_refs):
    for head, out_ref in enumerate(out_refs):
        out_ref[...] = block_ref[:, :, :, head * HD : (head + 1) * HD]


def pick_blocks(asked, memory_kv):
    head_block = pl.BlockSpec((1, 2, BLK, HD), lambda i, asked_ref: (i, 0, 0, 0))
    return pl.pallas_call(
        pick_kernel,
        grid_spec=pltpu.PrefetchScalarGridSpec(
            num_scalar_prefetch=1,
            grid=(OWNERS,),
            in_specs=[
                pl.BlockSpec((1, 2, BLK, WIDTH), lambda i, asked_ref: (asked_ref[i], 0, 0, 0))
            ],
            out_specs=[head_block] * HEADS,
        ),
        out_shape=[jax.ShapeDtypeStruct((OWNERS, 2, BLK, HD), jnp.bfloat16)] * HEADS,
        compiler_params=pltpu.CompilerParams(vmem_limit_bytes=VMEM_LIMIT),
        cost_estimate=pl.CostEstimate(
            flops=0, bytes_accessed=2 * OWNERS * 2 * BLK * WIDTH * 2, transcendentals=0
        ),
        name="pick_blocks",
    )(asked, memory_kv)


def project_kernel(y_ref, x_ref, w_ref, *refs):
    out_refs, (rows_scr, acc_scr) = refs[:YN], refs[YN:]
    step = pl.program_id(0)
    x_index, y_index = step // YN, step % YN

    @pl.when(y_index == 0)
    def _():
        for z in range(ZN):
            start = pl.multiple_of((z * XN + x_index) * BLK, BLK)
            rows_scr[:, z * BLK : (z + 1) * BLK] = x_ref[:, pl.ds(start, BLK)]

    part = dot(rows_scr[...], w_ref[...].reshape(ZN * BLK, WIDTH), ((1,), (0,)))

    @pl.when(x_index == 0)
    def _():
        acc_scr[y_index] = part

    @pl.when(x_index > 0)
    def _():
        acc_scr[y_index] += part

    @pl.when(step == XN * YN - 1)
    def _():
        for shift, out_ref in enumerate(out_refs):
            out_ref[...] = acc_scr[lax.rem(y_ref[0] + shift, YN)].astype(jnp.bfloat16)


def project(y_index, rows, w_all):
    whole = pl.BlockSpec((PAIR, WIDTH), lambda i, y_ref: (0, 0))
    return pl.pallas_call(
        project_kernel,
        grid_spec=pltpu.PrefetchScalarGridSpec(
            num_scalar_prefetch=1,
            grid=(XN * YN,),
            in_specs=[
                pl.BlockSpec((PAIR, DM), lambda i, y_ref: (0, 0)),
                pl.BlockSpec((1, ZN, BLK, WIDTH), lambda i, y_ref: (i, 0, 0, 0)),
            ],
            out_specs=[whole] * YN,
            scratch_shapes=[
                pltpu.VMEM((PAIR, ZN * BLK), jnp.bfloat16),
                pltpu.VMEM((YN, PAIR, WIDTH), jnp.float32),
            ],
        ),
        out_shape=[jax.ShapeDtypeStruct((PAIR, WIDTH), jnp.bfloat16)] * YN,
        compiler_params=pltpu.CompilerParams(vmem_limit_bytes=VMEM_LIMIT),
        cost_estimate=pl.CostEstimate(
            flops=2 * PAIR * DM * YN * WIDTH,
            bytes_accessed=2 * (PAIR * DM + DM * YN * WIDTH + PAIR * YN * WIDTH),
            transcendentals=0,
        ),
        name="project",
    )(y_index, rows, w_all)


def attend_kernel(owner_ref, y_ref, *refs):
    query_refs, refs = refs[:YN], refs[YN:]
    local_ref, memory_ref, grad_ref = refs[:3]
    att_ref, out_refs, (query_scr, back_scr) = refs[-YN - 3], refs[-YN - 2 : -2], refs[-2:]
    y_index = y_ref[0]
    score_scale = 1.0 / math.sqrt(HD)
    for shift, query_ref in enumerate(query_refs):
        query_scr[lax.rem(y_index + YN - shift, YN)] = query_ref[...]
    row = lax.broadcasted_iota(jnp.int32, (BLK, BLK), 0)
    col = lax.broadcasted_iota(jnp.int32, (BLK, BLK), 1)
    causal = row >= col
    for tile in range(TILES):
        rows = slice(tile * BLK, (tile + 1) * BLK)
        half = slice(tile % 2 * BLK, (tile % 2 + 1) * BLK)
        query = query_scr[tile // 2, half, :]
        grad = grad_ref[rows, :]
        owners = [owner_ref[tile, slot] for slot in range(TOPK)]
        keys = jnp.concatenate(
            [memory_ref[owner, 0] for owner in owners] + [local_ref[0, : (tile + 1) * BLK, :]]
        )
        values = jnp.concatenate(
            [memory_ref[owner, 1] for owner in owners] + [local_ref[1, : (tile + 1) * BLK, :]]
        )
        scores = dot(query, keys, ((1,), (1,))) * score_scale
        scores = jnp.concatenate(
            [scores[:, :-BLK], jnp.where(causal, scores[:, -BLK:], NEG_FILL)], axis=1
        )
        dprobs = dot(grad, values, ((1,), (1,)))
        row_max = jnp.max(scores, axis=1, keepdims=True)
        exps = jnp.exp(scores - row_max)
        probs = exps * (1.0 / jnp.sum(exps, axis=1, keepdims=True))
        attended = dot(probs.astype(jnp.bfloat16), values, ((1,), (0,)))
        att_ref[rows, :] = attended.astype(jnp.bfloat16)
        delta = jnp.sum(probs * dprobs, axis=1, keepdims=True)
        dscores = (probs * (dprobs - delta)).astype(jnp.bfloat16)
        back = dot(dscores, keys, ((1,), (0,))) * score_scale
        back_scr[tile // 2, half, :] = back.astype(jnp.bfloat16)
    for shift, out_ref in enumerate(out_refs):
        out_ref[...] = back_scr[lax.rem(y_index + shift, YN)]


def attend(head, owner_of, y_index, queries, local_kv, received, grad_out, attended):
    head_rows = pl.BlockSpec((CTX, HD), lambda i, *_: (0, head))
    part = pl.BlockSpec((PAIR, HD), lambda i, *_: (0, 0))
    operands = [*queries, local_kv, received, grad_out]
    in_specs = [pl.BlockSpec((PAIR, HD), lambda i, *_: (0, head))] * YN + [
        pl.BlockSpec((2, CTX, HD), lambda i, *_: (0, 0, head)),
        pl.BlockSpec((OWNERS, 2, BLK, HD), lambda i, *_: (0, 0, 0, 0)),
        head_rows,
    ]
    aliases = {}
    if attended is not None:
        operands.append(attended)
        in_specs.append(pl.BlockSpec(memory_space=pl.ANY))
        aliases = {len(operands) + 1: 0}
    keys_count = TILES * (TOPK * BLK) + BLK * TILES * (TILES + 1) // 2
    return pl.pallas_call(
        attend_kernel,
        grid_spec=pltpu.PrefetchScalarGridSpec(
            num_scalar_prefetch=2,
            grid=(1,),
            in_specs=in_specs,
            out_specs=[head_rows] + [part] * YN,
            scratch_shapes=[
                pltpu.VMEM((YN, PAIR, HD), jnp.bfloat16),
                pltpu.VMEM((YN, PAIR, HD), jnp.bfloat16),
            ],
        ),
        out_shape=[jax.ShapeDtypeStruct((CTX, WIDTH), jnp.bfloat16)]
        + [jax.ShapeDtypeStruct((PAIR, HD), jnp.bfloat16)] * YN,
        input_output_aliases=aliases,
        compiler_params=pltpu.CompilerParams(vmem_limit_bytes=VMEM_LIMIT),
        cost_estimate=pl.CostEstimate(
            flops=8 * BLK * keys_count * HD,
            bytes_accessed=2 * (OWNERS * 2 * BLK * HD + 6 * CTX * HD),
            transcendentals=BLK * keys_count,
        ),
        name="attend",
    )(owner_of, y_index, *operands)


def back_kernel(pos_ref, *refs):
    grad_refs, (w_ref, own_ref, send_ref) = refs[: YN * HEADS], refs[YN * HEADS :]
    x_index = pl.program_id(0)
    y_index, core = pos_ref[0], pos_ref[1]
    for out_ref, first in ((own_ref, core * BLK), (send_ref, (1 - core) * BLK)):
        rows = pl.ds(pl.multiple_of(first, BLK), BLK)
        total = jnp.zeros((BLK, ZN * BLK), jnp.float32)
        for shift in range(YN):
            grad = jnp.concatenate(
                [grad_refs[head * YN + shift][rows, :] for head in range(HEADS)], axis=1
            )
            weight = w_ref[lax.rem(y_index + YN - shift, YN)].reshape(ZN * BLK, WIDTH)
            total += dot(grad, weight, ((1,), (1,)))
        total = total.astype(out_ref.dtype)
        for z in range(ZN):
            start = pl.multiple_of((z * XN + x_index) * BLK, BLK)
            out_ref[:, pl.ds(start, BLK)] = total[:, z * BLK : (z + 1) * BLK]


def back_project(position, grads, w_all):
    part = pl.BlockSpec((PAIR, HD), lambda i, pos_ref: (0, 0))
    whole = pl.BlockSpec((BLK, DM), lambda i, pos_ref: (0, 0))
    return pl.pallas_call(
        back_kernel,
        grid_spec=pltpu.PrefetchScalarGridSpec(
            num_scalar_prefetch=1,
            grid=(XN,),
            in_specs=[part] * (YN * HEADS)
            + [pl.BlockSpec((YN, ZN, BLK, WIDTH), lambda i, pos_ref: (i, 0, 0, 0))],
            out_specs=[whole, whole],
        ),
        out_shape=[
            jax.ShapeDtypeStruct((BLK, DM), jnp.float32),
            jax.ShapeDtypeStruct((BLK, DM), jnp.bfloat16),
        ],
        compiler_params=pltpu.CompilerParams(vmem_limit_bytes=VMEM_LIMIT),
        cost_estimate=pl.CostEstimate(
            flops=2 * PAIR * DM * YN * WIDTH,
            bytes_accessed=2 * (2 * PAIR * DM + DM * YN * WIDTH),
            transcendentals=0,
        ),
        name="back_project",
    )(position, *grads, w_all)


def shift_y(array, shift):
    if shift == 0:
        return array
    return lax.ppermute(array, "y", [(i, (i + shift) % YN) for i in range(YN)])


def local(layer_input, w_query, local_kv, memory_kv, memory_ids, grad_out):
    y_index = lax.axis_index("y").astype(jnp.int32).reshape(1)
    core = lax.axis_index("c").astype(jnp.int32).reshape(1)
    me = lax.axis_index(MEM).astype(jnp.int32)
    all_ids = lax.all_gather(memory_ids, MEM, axis=0, tiled=True)
    all_ids = all_ids.reshape(OWNERS, TILES * TOPK)
    asked = jnp.max(jnp.where(all_ids // MB_DEV == me, all_ids % MB_DEV, 0), axis=1)
    outgoing = pick_blocks(asked, memory_kv)
    received = [
        lax.all_to_all(part, MEM, split_axis=0, concat_axis=0, tiled=True) for part in outgoing
    ]
    w_all = lax.all_gather(lax.all_gather(w_query, "z"), ("x", "y"))
    rows = lax.all_gather(layer_input, "c", axis=0, tiled=True)
    queries = project(y_index, rows, w_all)
    queries = [shift_y(part, shift) for shift, part in enumerate(queries)]
    owner_of = memory_ids // MB_DEV
    attended, grads = None, []
    for head in range(HEADS):
        attended, *parts = attend(
            head, owner_of, y_index, queries, local_kv, received[head], grad_out, attended
        )
        grads += [shift_y(part, shift) for shift, part in enumerate(parts)]
    own, send = back_project(jnp.concatenate([y_index, core]), grads, w_all)
    other = lax.ppermute(send, "c", [(0, 1), (1, 0)])
    return (attended, (own + other.astype(jnp.float32)).astype(jnp.bfloat16))


def solution(mesh):
    torus = Mesh(mesh.devices.reshape(ZN, XN, YN, CN), ("z", "x", "y", "c"))
    in_specs = (
        P(("z", "x", "y", "c"), None),
        P(MEM, ("y", "c")),
        P(None, MEM, ("y", "c")),
        P(MEM, None, None, ("y", "c")),
        P(MEM, None),
        P(MEM, ("y", "c")),
    )
    out_specs = (P(MEM, ("y", "c")), P(("z", "x", "y", "c"), None))
    return jax.shard_map(local, mesh=torus, in_specs=in_specs, out_specs=out_specs, check_vma=False)
```

time: 271 us -> 224 us (0.83); the launches traced: 268 us -> 223 us
  waiting for transfers between devices: 136 us -> 41.6 us
  blocking collectives: 23.1 us -> 95.9 us
  matrix products: 42.4 us -> 0 us
  Pallas kernels: 0 us -> 27.2 us
  starting transfers between devices: 9.71 us -> 25.7 us
  other arithmetic: 15.5 us -> 1.45 us
  local copies, waits for them, and re-layouts: 27 us -> 17.3 us
    all_to_all x1, waiting for transfers between devices: 90.9 us -> 0.01 us  [local(): lax.all_to_all(part, MEM, split_axis=0, concat_axis=0, tiled=True)]
    all_gather x1 -> x2, blocking collectives: 11.7 us -> 58.9 us  [the longest x1 37.4 us: local(): all_ids = lax.all_gather(memory_ids, MEM, axis=0, tiled=True)]
    reduce_scatter x1 -> x0, waiting for transfers between devices: 44.3 us -> none  [local(): lax.psum_scatter(lax.dot_general(grad_queries, weight_slice, (((1,), (1,)...]
    dot_general x10 -> x0, matrix products: 42.4 us -> none  [the longest x1 9.64 us: attend_context(): jnp.einsum('hqk,khd->qhd', loc_dscore, local_keys, preferred_element_type...]
    all_gather x2, waiting for transfers between devices: 0.01 us -> 30.9 us  [the longest x1 30.9 us: local(): w_all = lax.all_gather(lax.all_gather(w_query, 'z'), ('x', 'y'))]
    pallas_call x0 -> x5, Pallas kernels: none -> 27.2 us  [the longest x2 12.7 us: attend(): pl.pallas_call(attend_kernel, grid_spec=pltpu.PrefetchScalarGridSpec(num_...]
    all_to_all x1, blocking collectives: 11.4 us -> 36.9 us  [local(): lax.all_to_all(part, MEM, split_axis=0, concat_axis=0, tiled=True)]
    ppermute x0 -> x10, starting transfers between devices: none -> 16.8 us  [the longest x9 13 us: shift_y(): return lax.ppermute(array, 'y', [(i, (i + shift) % YN) for i in range(YN)])]
  transfers between devices with their start and end apart: 4 -> 13, of which waited for: 2 -> 7; matrix products, arithmetic and copies ran while one was open for 16% -> 0% of each run, Pallas kernels for 0% -> 6%
where the time goes in v1:
time: 224 us; the launch traced here: 223 us
  blocking collectives  95.9 us (43%)
  waiting for transfers between devices  41.6 us (19%)
  Pallas kernels  27.2 us (12%)
  starting transfers between devices  25.7 us (11%)
  local copies, waits for them, and re-layouts  17.3 us (8%)
  between operations  14.2 us (6%)
    all_gather x1, blocking collectives, local(): all_ids = lax.all_gather(memory_ids, MEM, axis=0, tiled=True)  37.4 us
    all_to_all x1, blocking collectives, local(): lax.all_to_all(part, MEM, split_axis=0, concat_axis=0, tiled=True)  36.9 us
    all_gather x1, waiting for transfers between devices, local(): w_all = lax.all_gather(lax.all_gather(w_query, 'z'), ('x', 'y'))  30.9 us
    all_gather x1, blocking collectives, local(): w_all = lax.all_gather(lax.all_gather(w_query, 'z'), ('x', 'y'))  21.6 us
    unnamed x44, local copies, waits for them, and re-layouts  17.2 us
    ppermute x9, starting transfers between devices, shift_y(): return lax.ppermute(array, 'y', [(i, (i + shift) % YN) for i in range(YN)])  13 us
    pallas_call x2, Pallas kernels, attend(): pl.pallas_call(attend_kernel, grid_spec=pltpu.PrefetchScalarGridSpec(num_...  12.7 us
    all_to_all x1, starting transfers between devices, local(): lax.all_to_all(part, MEM, split_axis=0, concat_axis=0, tiled=True)  8.87 us
  transfers between devices with their start and end apart: 13, of which 7 were waited for; matrix products, arithmetic and copies ran while one was open for 0% of the time, Pallas kernels for 6%

profile of v1, /device:TPU:129, one launch (start us, length us, event | category | flops | bytes accessed | tf_op | source)
XLA Modules:
  0.0 223.4 jit_solution(17945623879598757655)
XLA Ops:
  7.2 0.0 copy-start.20
  7.2 0.0 copy-start.2
  7.2 0.0 all-gather.6.cloned.1.call-start
  7.2 0.7 all-gather.6.cloned.1.call-update
  7.9 0.0 all-gather.8.cloned.1.call-start
  8.0 21.6 %all-gather = bf16[1024,256]{1,0:T(8,128)(2,1)} all-gather(bf16[128,256]{1,0:T(8,128)(2,1)} %param.7), channel_id=2, replica_groups=mesh['z'=8,'x'=4,'y'=4,'c'=2] {'z'}, dimensions={0}, use_global_device_ids=true | all-gather | bytes 589824 | tf_op jit(solution)/shard_map/all_gather | solution.py:257
  29.5 0.0 all-gather.8.cloned.1.call-update
  29.6 0.0 copy-done.20
  29.6 37.4 %all-gather.2 = s32[32,8,4]{1,2,0:T(4,128)S(1)} all-gather(s32[1,8,4]{1,2,0:T(4,128)S(1)} %bitcast.10), channel_id=1, replica_groups=mesh['z'=8,'x'=4,'y'=4,'c'=2] {'z','x'}, dimensions={0}, use_global_device_ids=true | all-gather | bytes 4224 | tf_op jit(solution)/shard_map/all_gather | solution.py:250
  67.0 0.1 reshape.17
  67.1 0.1 reduce_max.14
  67.2 0.1 reduce_max.18.asked_ref
  67.3 0.0 copy-done.2
  67.3 1.7 pick_blocks.1
  69.0 0.0 copy-start.3
  69.0 36.9 %all_to_all.10.refs_5_ = bf16[32,2,128,128]{3,2,1,0:T(8,128)(2,1)} all-to-all(bf16[32,2,128,128]{3,2,1,0:T(8,128)(2,1)S(1)} %get-tuple-element.25), channel_id=1, replica_groups=mesh['z'=8,'x'=4,'y'=4,'c'=2] {'z','x'}, dimensions={0} | all-to-all | bytes 4194304 | tf_op jit(solution)/shard_map/all_to_all | solution.py:255
  106.0 0.0 copy-done.3
  106.0 8.9 %all-to-all-start = ((bf16[32,2,128,128]{3,2,1,0:T(8,128)(2,1)}), bf16[32,2,128,128]{3,2,1,0:T(8,128)(2,1)S(1)}, u32[]{:S(2)}, u32[]{:S(2)}) async-start(bf16[32,2,128,128]{3,2,1,0:T(8,128)(2,1)} %copy-done.3), calls=%async_computation | async-start | bytes 4194304 | tf_op jit(solution)/shard_map/all_to_all | solution.py:255
  114.9 0.1 copy.18
  114.9 30.9 %all-gather.8.cloned.1.call-done = bf16[128,128,256]{2,1,0:T(8,128)(2,1)} async-done(((bf16[8,128,256]{2,1,0:T(8,128)(2,1)}), bf16[128,128,256]{2,1,0:T(8,128)(2,1)}) %all-gather.8.cloned.1.call-update) | async-done | bytes 8388624 | tf_op jit(solution)/shard_map/all_gather | solution.py:257
  145.9 3.4 %copy-done = bf16[128,128,256]{2,1,0:T(8,128)(2,1)S(1)} copy-done((bf16[128,128,256]{2,1,0:T(8,128)(2,1)S(1)}, bf16[128,128,256]{2,1,0:T(8,128)(2,1)}, u32[]{:S(2)}) %copy-start) | copy-done | bytes 8388632
  149.2 1.6 copy-done.5
  150.8 6.1 %project.1 = (bf16[256,256]{1,0:T(8,128)(2,1)S(1)}, bf16[256,256]{1,0:T(8,128)(2,1)S(1)}, bf16[256,256]{1,0:T(8,128)(2,1)S(1)}, bf16[256,256]{1,0:T(8,128)(2,1)S(1)}) custom-call(s32[1]{0:T(128)} %bitcast.y_ref, bf16[256,4096]{1,0:T(8,128)(2,1)S(1)} %copy-done.5, bf16[16,8,128,256]{3,2,1,0:T(8,128)(2,1)S(1)} %bitcast.7), custom_call_target="tpu_custom_call" | custom-call | flops 2147483648 | bytes 11010048 | tf_op jit(solution)/shard_map/project/pallas_call | solution.py:88
  157.0 2.2 collective-permute-start
  159.2 2.4 %collective-permute-start.1 = (bf16[256,256]{1,0:T(8,128)(2,1)S(1)}, bf16[256,256]{1,0:T(8,128)(2,1)S(1)}, u32[]{:S(2)}, u32[]{:S(2)}) collective-permute-start(bf16[256,256]{1,0:T(8,128)(2,1)S(1)} %get-tuple-element.22), channel_id=1, source_target_pairs={{0,4},{2,6},{4,0},{6,2},{1,5},{3,7},{5,1},{7,3},{8,12},{10,14},{12... | collective-permute-start | bytes 393224 | tf_op jit(solution)/shard_map/ppermute | solution.py:243
  161.6 1.2 collective-permute-start.2
  162.8 0.9 collective-permute-done.refs_1_
  163.6 3.7 %collective-permute-done.1.refs_2_ = bf16[256,256]{1,0:T(8,128)(2,1)S(1)} collective-permute-done((bf16[256,256]{1,0:T(8,128)(2,1)S(1)}, bf16[256,256]{1,0:T(8,128)(2,1)S(1)}, u32[]{:S(2)}, u32[]{:S(2)}) %collective-permute-start.1) | collective-permute-done | bytes 131104 | tf_op jit(solution)/shard_map/ppermute | solution.py:243
  167.3 0.0 collective-permute-done.2.refs_3_
  167.3 0.0 copy-done.4
  167.3 0.0 copy-done.6
  167.3 6.3 %attend.2 = (bf16[1024,256]{1,0:T(8,128)(2,1)}, bf16[256,128]{1,0:T(8,128)(2,1)S(1)}, bf16[256,128]{1,0:T(8,128)(2,1)S(1)}, bf16[256,128]{1,0:T(8,128)(2,1)S(1)}, bf16[256,128]{1,0:T(8,128)(2,1)S(1)}) custom-call(s32[8,4]{1,0:T(8,128)S(1)} %add_select_fusion.2.owner_ref, s32[1]{0:T(128)} %bitcast.y_ref, bf16[256,256]{1,0:T(8,128)(2,1)S(1)} %get-tuple-element.20.refs_0_, ...), custom_call_target="tpu_custom_call" | custom-call | flops 1140850688 | bytes 3670016 | tf_op jit(solution)/shard_map/attend/pallas_call | solution.py:170
  173.7 0.7 copy-done.9
  174.3 0.6 copy-done.11
  175.0 0.6 copy-done.15
  175.6 0.6 copy-done.16
  176.2 0.6 copy-done.17
  176.8 0.0 all-to-all-done.refs_5_
  176.8 1.0 copy-done.8
  177.9 0.9 copy-done.10
  178.8 6.4 %attend.3 = (bf16[1024,256]{1,0:T(8,128)(2,1)}, bf16[256,128]{1,0:T(8,128)(2,1)S(1)}, bf16[256,128]{1,0:T(8,128)(2,1)}, bf16[256,128]{1,0:T(8,128)(2,1)S(1)}, bf16[256,128]{1,0:T(8,128)(2,1)S(1)}) custom-call(s32[8,4]{1,0:T(8,128)S(1)} %add_select_fusion.2.owner_ref, s32[1]{0:T(128)} %bitcast.y_ref, ...), custom_call_target="tpu_custom_call", output_to_operand_aliasing={{0}: (9, {})} | custom-call | flops 1140850688 | bytes 3670016 | tf_op jit(solution)/shard_map/attend/pallas_call | solution.py:170
  185.2 0.6 copy-done.13
  185.8 0.6 copy-done.18
  186.4 0.6 copy-done.19
  187.1 0.8 collective-permute-start.6
  187.9 2.5 %collective-permute-start.7 = (bf16[256,128]{1,0:T(8,128)(2,1)}, bf16[256,128]{1,0:T(8,128)(2,1)S(1)}, u32[]{:S(2)}, u32[]{:S(2)}) collective-permute-start(bf16[256,128]{1,0:T(8,128)(2,1)} %copy-done.19), channel_id=1, source_target_pairs={{0,4},{2,6},{4,0},{6,2},{1,5},{3,7},{5,1},{7,3},{8,12},{10,14},{12... | collective-permute-start | bytes 196616 | tf_op jit(solution)/shard_map/ppermute | solution.py:243
  190.4 0.9 collective-permute-start.8
  191.2 0.6 collective-permute-start.3
  191.8 0.6 collective-permute-start.4
  192.4 0.0 collective-permute-done.6.refs_5_
  192.4 1.8 collective-permute-start.5
  194.2 0.1 pad_add_fusion.pos_ref
  194.3 0.0 collective-permute-done.7.refs_6_
  194.3 0.0 collective-permute-done.8.refs_7_
  194.3 2.4 %collective-permute-done.3.refs_1_ = bf16[256,128]{1,0:T(8,128)(2,1)S(1)} collective-permute-done((bf16[256,128]{1,0:T(8,128)(2,1)}, bf16[256,128]{1,0:T(8,128)(2,1)S(1)}, u32[]{:S(2)}, u32[]{:S(2)}) %collective-permute-start.3) | collective-permute-done | bytes 65568 | tf_op jit(solution)/shard_map/ppermute | solution.py:243
  196.7 0.3 collective-permute-done.4.refs_2_
  196.9 0.5 collective-permute-done.5.refs_3_
  197.4 3.4 %copy-done.1 = bf16[128,128,256]{2,1,0:T(8,128)(2,1)S(1)} copy-done((bf16[128,128,256]{2,1,0:T(8,128)(2,1)S(1)}, bf16[128,128,256]{2,1,0:T(8,128)(2,1)}, u32[]{:S(2)}) %copy-start.1) | copy-done | bytes 8388632
  200.8 0.8 copy-done.12
  201.6 0.8 copy-done.14
  202.5 6.7 %back_project.1 = (f32[128,4096]{1,0:T(8,128)S(1)}, bf16[128,4096]{1,0:T(8,128)(2,1)S(1)}) custom-call(s32[2]{0:T(128)S(1)} %pad_add_fusion.pos_ref, bf16[256,128]{1,0:T(8,128)(2,1)S(1)} %copy-done.12, bf16[256,128]{1,0:T(8,128)(2,1)S(1)} %collective-permute-done.3.refs_1_, bf16[256,128]{1,0:T(8,128)(2,1)S(1)} %collective-permute-done.4.refs_2_, ...), custom_call_target="tpu_custom_call" | custom-call | flops 2147483648 | bytes 12582912 | tf_op jit(solution)/shard_map/back_project/pallas_call | solution.py:217
  209.2 3.8 %collective-permute-start.9 = (bf16[128,4096]{1,0:T(8,128)(2,1)S(1)}, bf16[128,4096]{1,0:T(8,128)(2,1)S(1)}, u32[]{:S(2)}, u32[]{:S(2)}) collective-permute-start(bf16[128,4096]{1,0:T(8,128)(2,1)S(1)} %get-tuple-element.37), channel_id=1, source_target_pairs={{0,1},{1,0},{2,3},{3,2},{4,5},{5,4},{6,7},{7,6},{8,9},{9,8},{10,11... | collective-permute-start | bytes 3145736 | tf_op jit(solution)/shard_map/ppermute | solution.py:269
  213.0 2.3 %collective-permute-done.9 = bf16[128,4096]{1,0:T(8,128)(2,1)S(1)} collective-permute-done((bf16[128,4096]{1,0:T(8,128)(2,1)S(1)}, bf16[128,4096]{1,0:T(8,128)(2,1)S(1)}, u32[]{:S(2)}, u32[]{:S(2)}) %collective-permute-start.9) | collective-permute-done | bytes 1048608 | tf_op jit(solution)/shard_map/ppermute | solution.py:269
  215.3 1.2 add_convert_fusion
  (23 shorter events, 0.1 us)
Async XLA Ops:
  7.2 22.4 %copy-start.20 = (s32[8,4]{0,1:T(4,128)S(1)}, s32[8,4]{0,1:T(4,128)}, u32[]{:S(2)}) copy-start(s32[8,4]{0,1:T(4,128)} %param.10) | copy-start | bytes 388
  7.2 60.1 %copy-start.2 = (bf16[16,2,128,256]{3,2,1,0:T(8,128)(2,1)S(1)}, bf16[16,2,128,256]{3,2,1,0:T(8,128)(2,1)}, u32[]{:S(2)}) copy-start(bf16[16,2,128,256]{3,2,1,0:T(8,128)(2,1)} %block_ref.1) | copy-start | bytes 6291460
  7.2 107.8 %all-gather.6.cloned.1.call-start = ((), (), s32[]{:S(2)}) async-start(), calls=%async_computation.2 | async-start | bytes 3145728 | tf_op jit(solution)/shard_map/all_gather | solution.py:258
  7.9 137.9 %all-gather.8.cloned.1.call-start = ((), (), s32[]{:S(2)}) async-start(), calls=%async_computation.3 | async-start | bytes 8912896 | tf_op jit(solution)/shard_map/all_gather | solution.py:257
  69.0 36.9 %copy-start.3 = (bf16[32,2,128,128]{3,2,1,0:T(8,128)(2,1)}, bf16[32,2,128,128]{3,2,1,0:T(8,128)(2,1)S(1)}, u32[]{:S(2)}) copy-start(bf16[32,2,128,128]{3,2,1,0:T(8,128)(2,1)S(1)} %get-tuple-element.24) | copy-start | bytes 6291460
  106.0 70.9 %all-to-all-start = ((bf16[32,2,128,128]{3,2,1,0:T(8,128)(2,1)}), bf16[32,2,128,128]{3,2,1,0:T(8,128)(2,1)S(1)}, u32[]{:S(2)}, u32[]{:S(2)}) async-start(bf16[32,2,128,128]{3,2,1,0:T(8,128)(2,1)} %copy-done.3), calls=%async_computation | async-start | bytes 4194304 | tf_op jit(solution)/shard_map/all_to_all | solution.py:255
  145.9 3.4 %copy-start = (bf16[128,128,256]{2,1,0:T(8,128)(2,1)S(1)}, bf16[128,128,256]{2,1,0:T(8,128)(2,1)}, u32[]{:S(2)}) copy-start(bf16[128,128,256]{2,1,0:T(8,128)(2,1)} %all-gather.8.cloned.1.call-done) | copy-start | bytes 25165828
  149.2 1.6 copy-start.5
  150.8 16.5 %copy-start.4 = (bf16[32,2,128,128]{3,2,1,0:T(8,128)(2,1)S(1)}, bf16[32,2,128,128]{3,2,1,0:T(8,128)(2,1)}, u32[]{:S(2)}) copy-start(bf16[32,2,128,128]{3,2,1,0:T(8,128)(2,1)} %all_to_all.10.refs_5_) | copy-start | bytes 6291460
  150.8 16.5 %copy-start.6 = (bf16[2,1024,256]{2,1,0:T(8,128)(2,1)S(1)}, bf16[2,1024,256]{2,1,0:T(8,128)(2,1)}, u32[]{:S(2)}) copy-start(bf16[2,1024,256]{2,1,0:T(8,128)(2,1)} %refs_4_.3) | copy-start | bytes 3145732
  150.8 16.5 %copy-start.7 = (bf16[1024,256]{1,0:T(8,128)(2,1)S(1)}, bf16[1024,256]{1,0:T(8,128)(2,1)}, u32[]{:S(2)}) copy-start(bf16[1024,256]{1,0:T(8,128)(2,1)} %refs_6_.3) | copy-start | bytes 1572868
  157.0 6.7 %collective-permute-start = (bf16[256,256]{1,0:T(8,128)(2,1)S(1)}, bf16[256,256]{1,0:T(8,128)(2,1)S(1)}, u32[]{:S(2)}, u32[]{:S(2)}) collective-permute-start(bf16[256,256]{1,0:T(8,128)(2,1)S(1)} %get-tuple-element.21), channel_id=1, source_target_pairs={{0,2},{2,4},{4,6},{6,0},{1,3},{3,5},{5,7},{7,1},{8,10},{10,12},{12... | collective-permute-start | bytes 393224 | tf_op jit(solution)/shard_map/ppermute | solution.py:243
  159.2 8.1 %collective-permute-start.1 = (bf16[256,256]{1,0:T(8,128)(2,1)S(1)}, bf16[256,256]{1,0:T(8,128)(2,1)S(1)}, u32[]{:S(2)}, u32[]{:S(2)}) collective-permute-start(bf16[256,256]{1,0:T(8,128)(2,1)S(1)} %get-tuple-element.22), channel_id=1, source_target_pairs={{0,4},{2,6},{4,0},{6,2},{1,5},{3,7},{5,1},{7,3},{8,12},{10,14},{12... | collective-permute-start | bytes 393224 | tf_op jit(solution)/shard_map/ppermute | solution.py:243
  161.6 5.7 %collective-permute-start.2 = (bf16[256,256]{1,0:T(8,128)(2,1)S(1)}, bf16[256,256]{1,0:T(8,128)(2,1)S(1)}, u32[]{:S(2)}, u32[]{:S(2)}) collective-permute-start(bf16[256,256]{1,0:T(8,128)(2,1)S(1)} %get-tuple-element.23), channel_id=1, source_target_pairs={{0,6},{2,0},{4,2},{6,4},{1,7},{3,1},{5,3},{7,5},{8,14},{10,8},{12,... | collective-permute-start | bytes 393224 | tf_op jit(solution)/shard_map/ppermute | solution.py:243
  173.7 0.7 copy-start.9
  174.3 0.6 copy-start.11
  175.0 0.6 copy-start.15
  175.6 0.6 copy-start.16
  176.2 0.6 copy-start.17
  176.8 1.0 copy-start.8
  177.9 0.9 copy-start.10
  185.2 0.6 copy-start.13
  185.8 0.6 copy-start.18
  186.4 0.6 copy-start.19
  187.1 5.4 %collective-permute-start.6 = (bf16[256,128]{1,0:T(8,128)(2,1)}, bf16[256,128]{1,0:T(8,128)(2,1)S(1)}, u32[]{:S(2)}, u32[]{:S(2)}) collective-permute-start(bf16[256,128]{1,0:T(8,128)(2,1)} %get-tuple-element.33), channel_id=1, source_target_pairs={{0,2},{2,4},{4,6},{6,0},{1,3},{3,5},{5,7},{7,1},{8,10},{10,12},{12... | collective-permute-start | bytes 196616 | tf_op jit(solution)/shard_map/ppermute | solution.py:243
  187.9 6.4 %collective-permute-start.7 = (bf16[256,128]{1,0:T(8,128)(2,1)}, bf16[256,128]{1,0:T(8,128)(2,1)S(1)}, u32[]{:S(2)}, u32[]{:S(2)}) collective-permute-start(bf16[256,128]{1,0:T(8,128)(2,1)} %copy-done.19), channel_id=1, source_target_pairs={{0,4},{2,6},{4,0},{6,2},{1,5},{3,7},{5,1},{7,3},{8,12},{10,14},{12... | collective-permute-start | bytes 196616 | tf_op jit(solution)/shard_map/ppermute | solution.py:243
  190.4 3.9 %collective-permute-start.8 = (bf16[256,128]{1,0:T(8,128)(2,1)}, bf16[256,128]{1,0:T(8,128)(2,1)S(1)}, u32[]{:S(2)}, u32[]{:S(2)}) collective-permute-start(bf16[256,128]{1,0:T(8,128)(2,1)} %copy-done.18), channel_id=1, source_target_pairs={{0,6},{2,0},{4,2},{6,4},{1,7},{3,1},{5,3},{7,5},{8,14},{10,8},{12,... | collective-permute-start | bytes 196616 | tf_op jit(solution)/shard_map/ppermute | solution.py:243
  191.2 5.4 %collective-permute-start.3 = (bf16[256,128]{1,0:T(8,128)(2,1)}, bf16[256,128]{1,0:T(8,128)(2,1)S(1)}, u32[]{:S(2)}, u32[]{:S(2)}) collective-permute-start(bf16[256,128]{1,0:T(8,128)(2,1)} %copy-done.17), channel_id=1, source_target_pairs={{0,2},{2,4},{4,6},{6,0},{1,3},{3,5},{5,7},{7,1},{8,10},{10,12},{12... | collective-permute-start | bytes 196616 | tf_op jit(solution)/shard_map/ppermute | solution.py:243
  191.8 5.1 %collective-permute-start.4 = (bf16[256,128]{1,0:T(8,128)(2,1)}, bf16[256,128]{1,0:T(8,128)(2,1)S(1)}, u32[]{:S(2)}, u32[]{:S(2)}) collective-permute-start(bf16[256,128]{1,0:T(8,128)(2,1)} %copy-done.16), channel_id=1, source_target_pairs={{0,4},{2,6},{4,0},{6,2},{1,5},{3,7},{5,1},{7,3},{8,12},{10,14},{12... | collective-permute-start | bytes 196616 | tf_op jit(solution)/shard_map/ppermute | solution.py:243
  192.4 5.0 %collective-permute-start.5 = (bf16[256,128]{1,0:T(8,128)(2,1)}, bf16[256,128]{1,0:T(8,128)(2,1)S(1)}, u32[]{:S(2)}, u32[]{:S(2)}) collective-permute-start(bf16[256,128]{1,0:T(8,128)(2,1)} %copy-done.15), channel_id=1, source_target_pairs={{0,6},{2,0},{4,2},{6,4},{1,7},{3,1},{5,3},{7,5},{8,14},{10,8},{12,... | collective-permute-start | bytes 196616 | tf_op jit(solution)/shard_map/ppermute | solution.py:243
  197.4 3.4 %copy-start.1 = (bf16[128,128,256]{2,1,0:T(8,128)(2,1)S(1)}, bf16[128,128,256]{2,1,0:T(8,128)(2,1)}, u32[]{:S(2)}) copy-start(bf16[128,128,256]{2,1,0:T(8,128)(2,1)} %all-gather.8.cloned.1.call-done) | copy-start | bytes 25165828
  200.8 0.8 copy-start.12
  201.6 0.8 copy-start.14
  209.2 6.1 %collective-permute-start.9 = (bf16[128,4096]{1,0:T(8,128)(2,1)S(1)}, bf16[128,4096]{1,0:T(8,128)(2,1)S(1)}, u32[]{:S(2)}, u32[]{:S(2)}) collective-permute-start(bf16[128,4096]{1,0:T(8,128)(2,1)S(1)} %get-tuple-element.37), channel_id=1, source_target_pairs={{0,1},{1,0},{2,3},{3,2},{4,5},{5,4},{6,7},{7,6},{8,9},{9,8},{10,11... | collective-permute-start | bytes 3145736 | tf_op jit(solution)/shard_map/ppermute | solution.py:269
Sparse Core Ops, SparseCore 0:
  9.8 17.8 all-gather.5
  30.2 115.6 all-gather.7
